TPU v7x, 32 devices: a whole 2x2x4 slice. The times are simulated.
32 devices in a mesh: row: 8 (over z, x), col: 4 (over y, core).
Axes of the slice: x: 2, y: 2, z: 4, core: 2. Of those that a mesh axis runs over, the one named last changes fastest.
Arguments:
- points: float32 [2, 2048], P(None, 'row'), may hold values from 0 to 1, as said below
- strip_ids: int32 [2048], P('row'), may hold values from 0 to 3, as said below
- counts: int32 [8], P('row'), may hold values from 128 to 256, as said below
- mode_index: int32 [1024], P('col'), may hold values from 0 to 32767, as said below
- reflectors: float32 [2048, 512], P('row'), may hold values from -0.125 to 0.125
Outputs:
- block_out: float32 [2048, 2048], P('row', 'col')
- upper_out: float32 [128, 2048], P(None, 'col')
Inputs may be any that keep to these rules, and one draw needn't show every extreme that they name: `counts`: an owner's live slots come first among its 256 slots; some owner has all 256 live. `mode_index`: the modes are distinct. `points`: every point lies in the triangle x >= 0, y >= 0, x + y <= 1. `strip_ids`: A slot of owner o has strip o * 4 // 8 or one more, at most 3.
All inputs are finite; a program needn't handle non-finite values.
Results may differ from a plain program's by a relative error of at most 0.0003.
Values sent between devices are 32-bit elements; how exact they have to be, the bound alone decides.
A program may use at most 64 MiB of HBM per device.

v0:
```python
import jax
import jax.numpy as jnp
from jax import lax
from jax.sharding import PartitionSpec as P

PANEL = 128
STRIPS = 4


PRECISE = lax.Precision.HIGHEST
SHIFT_RATE = 1e-06


def spread(array, axis, root):
    mine = lax.axis_index(axis) == root
    return lax.psum(jnp.where(mine, array, jnp.zeros_like(array)), axis)


def product(left, right):
    return jnp.dot(left, right, precision=PRECISE, preferred_element_type=jnp.float32)


def transposed_product(left, right):
    return lax.dot_general(
        left, right, (((0,), (0,)), ((), ())), precision=PRECISE, preferred_element_type=jnp.float32
    )


def cholesky_lower(gram):
    order_ids = jnp.arange(gram.shape[0], dtype=jnp.int32)

    def column_step(column, lower):
        row_now = lax.dynamic_index_in_dim(lower, column, 0, keepdims=False)
        target = lax.dynamic_index_in_dim(gram, column, 1, keepdims=False) - product(lower, row_now)
        pivot = jnp.sqrt(lax.dynamic_index_in_dim(target, column, 0, keepdims=False))
        new_column = jnp.where(order_ids >= column, target / pivot, jnp.zeros_like(target))
        return lax.dynamic_update_slice_in_dim(lower, new_column[:, None], column, 1)

    return lax.fori_loop(0, gram.shape[0], column_step, jnp.zeros_like(gram))


def lower_inverse(lower):
    order_ids = jnp.arange(lower.shape[0], dtype=jnp.int32)

    def row_step(row, inverse):
        row_now = lax.dynamic_index_in_dim(lower, row, 0, keepdims=False)
        unit_row = (order_ids == row).astype(lower.dtype)
        pivot = lax.dynamic_index_in_dim(row_now, row, 0, keepdims=False)
        new_row = (unit_row - product(row_now, inverse)) / pivot
        return lax.dynamic_update_slice_in_dim(inverse, new_row[None, :], row, 0)

    return lax.fori_loop(0, lower.shape[0], row_step, jnp.zeros_like(lower))


def assemble(points, strip_ids, live_mask, mode_index):
    freq_x = (mode_index // 128 - 128).astype(jnp.float32)
    freq_y = (mode_index % 128 + 1).astype(jnp.float32)
    phases = jnp.pi * (points[0][:, None] * freq_x[None, :] + points[1][:, None] * freq_y[None, :])
    weight = 3.0 * jnp.power(10.0, -strip_ids.astype(jnp.float32) / (STRIPS - 1)) * live_mask
    columns_all = jnp.stack([jnp.cos(phases), jnp.sin(phases)], axis=-1).reshape(
        phases.shape[0], -1
    )
    return columns_all * weight[:, None]


def reflect(gram_block, coeffs):
    upper_factor = jnp.triu(gram_block, 1) + 0.5 * jnp.diag(jnp.diagonal(gram_block))
    return product(lower_inverse(upper_factor.T), coeffs)


def orthonormalize(panel_cols):
    gram_one = lax.psum(transposed_product(panel_cols, panel_cols), "row")
    shift_size = SHIFT_RATE * jnp.trace(gram_one)
    lower_one = cholesky_lower(gram_one + shift_size * jnp.eye(PANEL, dtype=jnp.float32))
    basis_one = product(panel_cols, lower_inverse(lower_one).T)
    gram_two = lax.psum(transposed_product(basis_one, basis_one), "row")
    lower_two = cholesky_lower(gram_two)
    basis_cols = product(basis_one, lower_inverse(lower_two).T)
    return (basis_cols, lower_one.T)


def on_device(points, strip_ids, counts, mode_index, reflectors):
    row_count = points.shape[1]
    live_mask = (jnp.arange(row_count, dtype=jnp.int32) < counts[0]).astype(jnp.float32)
    work_block = assemble(points, strip_ids, live_mask, mode_index)
    stored = reflectors * live_mask[:, None]
    panels = stored.shape[1] // PANEL
    shaped = stored.reshape(row_count, panels, PANEL)
    gram_blocks = jnp.einsum(
        "rkp,rkq->kpq", shaped, shaped, precision=PRECISE, preferred_element_type=jnp.float32
    )
    gram_blocks = lax.psum(gram_blocks, "row")

    def apply_panel(panel_step, current):
        columns = lax.dynamic_slice_in_dim(stored, panel_step * PANEL, PANEL, 1)
        coeffs = lax.psum(transposed_product(columns, current), "row")
        gram_block = lax.dynamic_index_in_dim(gram_blocks, panel_step, 0, keepdims=False)
        return current - product(columns, reflect(gram_block, coeffs))

    work_block = lax.fori_loop(0, panels, apply_panel, work_block)
    basis_cols, factor = orthonormalize(work_block[:, :PANEL])
    basis_cols = spread(basis_cols, "col", 0)
    tail_rows = lax.psum(transposed_product(basis_cols, work_block), "row")
    remainder = work_block - product(basis_cols, tail_rows)
    col_count = work_block.shape[1]
    global_col = lax.axis_index("col") * col_count + jnp.arange(col_count, dtype=jnp.int32)
    is_panel = (global_col < PANEL)[None, :]
    norm_scale = jnp.sqrt(jnp.float32(row_count * lax.axis_size("row")))
    padded_basis = jnp.pad(basis_cols, ((0, 0), (0, col_count - PANEL)))
    padded_factor = jnp.pad(factor, ((0, 0), (0, col_count - PANEL)))
    block_out = jnp.where(is_panel, padded_basis * norm_scale, remainder)
    upper_out = jnp.where(is_panel, padded_factor, tail_rows) / norm_scale
    return (block_out, upper_out)


def solution(mesh):
    return jax.shard_map(
        on_device,
        mesh=mesh,
        in_specs=(P(None, "row"), P("row"), P("row"), P("col"), P("row", None)),
        out_specs=(P("row", "col"), P(None, "col")),
        check_vma=False,
    )
```

profile of v0, /device:TPU:0, one launch (start us, length us, event | category | flops | bytes accessed | tf_op | source)
XLA Modules:
  0.0 2036.4 jit_solution(15213815674457690325)
XLA Ops:
  7.9 3.0 fusion.44
  12.3 1.1 fusion.48
  15.9 69.3 %all-reduce.9.cloned.1.call-done = f32[4,128,128]{2,1,0:T(8,128)} async-done(((f32[4,128,128]{2,1,0:T(8,128)}), f32[4,128,128]{2,1,0:T(8,128)}) %all-reduce.9.cloned.1.call-update) | async-done | bytes 262160 | tf_op jit(solution)/shard_map/psum | solution.py:92
  85.2 805.3 %while.115 = (s32[]{:T(128)}, f32[256,512]{1,0:T(8,128)S(1)}, f32[256,512]{1,0:T(8,128)S(1)}, f32[4,128,128]{2,1,0:T(8,128)}, s32[]{:T(128)}, /*index=5*/s32[]{:...) while((s32[]{:T(128)}, f32[256,512]{1,0:T(8,128)S(1)}, ...), condition=%wide.region_5.6_spmd, body=%wide.region_1.5_spmd.sunk | while | flops 503809024 | bytes 5053304 | solution.py:100
  85.3 1.2 fusion.112
  87.4 1.3 gather_fusion
  88.7 195.8 %while.120 = (s32[]{:T(128)}, f32[128,128]{1,0:T(8,128)S(1)}, f32[128,128]{1,0:T(8,128)S(1)}, s32[]{:T(128)}, s32[]{:T(128)}, /*index=5*/s32[]{:T(128)}) while((s32[]{:T(128)}, f32[128,128]{1,0:T(8,128)S(1)}, f32[128,128]{1,0:T(8,128)S(1)}, s32[]{:T(128)}, s32[]{:T(128)}, /*index=5*/s32[]{:T(128)}) %tuple.222), condition=%wide.region_3.3_spmd.clone, body=%wide.region_2.2_spmd.clone.sunk | while | flops 197123 | bytes 69221 | solution.py:52
  284.5 1.3 fusion.113
  286.6 1.2 fusion.112
  288.7 1.3 gather_fusion
  290.1 195.8 %while.120 = (s32[]{:T(128)}, f32[128,128]{1,0:T(8,128)S(1)}, f32[128,128]{1,0:T(8,128)S(1)}, s32[]{:T(128)}, s32[]{:T(128)}, /*index=5*/s32[]{:T(128)}) while((s32[]{:T(128)}, f32[128,128]{1,0:T(8,128)S(1)}, f32[128,128]{1,0:T(8,128)S(1)}, s32[]{:T(128)}, s32[]{:T(128)}, /*index=5*/s32[]{:T(128)}) %tuple.222), condition=%wide.region_3.3_spmd.clone, body=%wide.region_2.2_spmd.clone.sunk | while | flops 197123 | bytes 69221 | solution.py:52
  485.9 1.3 fusion.113
  487.9 1.2 fusion.112
  490.1 1.3 gather_fusion
  491.4 195.8 %while.120 = (s32[]{:T(128)}, f32[128,128]{1,0:T(8,128)S(1)}, f32[128,128]{1,0:T(8,128)S(1)}, s32[]{:T(128)}, s32[]{:T(128)}, /*index=5*/s32[]{:T(128)}) while((s32[]{:T(128)}, f32[128,128]{1,0:T(8,128)S(1)}, f32[128,128]{1,0:T(8,128)S(1)}, s32[]{:T(128)}, s32[]{:T(128)}, /*index=5*/s32[]{:T(128)}) %tuple.222), condition=%wide.region_3.3_spmd.clone, body=%wide.region_2.2_spmd.clone.sunk | while | flops 197123 | bytes 69221 | solution.py:52
  687.2 1.3 fusion.113
  689.3 1.2 fusion.112
  691.4 1.3 gather_fusion
  692.8 195.8 %while.120 = (s32[]{:T(128)}, f32[128,128]{1,0:T(8,128)S(1)}, f32[128,128]{1,0:T(8,128)S(1)}, s32[]{:T(128)}, s32[]{:T(128)}, /*index=5*/s32[]{:T(128)}) while((s32[]{:T(128)}, f32[128,128]{1,0:T(8,128)S(1)}, f32[128,128]{1,0:T(8,128)S(1)}, s32[]{:T(128)}, s32[]{:T(128)}, /*index=5*/s32[]{:T(128)}) %tuple.222), condition=%wide.region_3.3_spmd.clone, body=%wide.region_2.2_spmd.clone.sunk | while | flops 197123 | bytes 69221 | solution.py:52
  888.6 1.3 fusion.113
  890.6 1.0 fusion.51
  891.7 71.6 %all-reduce.11.cloned.1.call-done = f32[128,128]{1,0:T(8,128)} async-done(((f32[128,128]{1,0:T(8,128)}), f32[128,128]{1,0:T(8,128)}) %all-reduce.11.cloned.1.call-update) | async-done | bytes 65552 | tf_op jit(solution)/shard_map/psum | solution.py:72
  963.3 1.5 select_reduce_fusion
  965.6 257.4 %while.116 = (s32[]{:T(128)}, f32[128,128]{1,0:T(8,128)S(1)}, f32[128,128]{0,1:T(8,128)S(1)}, s32[]{:T(128)}, s32[]{:T(128)}) while((s32[]{:T(128)}, f32[128,128]{1,0:T(8,128)S(1)}, f32[128,128]{0,1:T(8,128)S(1)}, s32[]{:T(128)}, s32[]{:T(128)}) %tuple.228), condition=%wide.region_9.10_spmd.clone, body=%wide.region_8.9_spmd.clone.sunk | while | flops 197122 | bytes 71261 | solution.py:39
  1223.0 184.3 %while.117 = (s32[]{:T(128)}, f32[128,128]{1,0:T(8,128)S(1)}, f32[128,128]{1,0:T(8,128)S(1)}, s32[]{:T(128)}, s32[]{:T(128)}, /*index=5*/s32[]{:T(128)}) while((s32[]{:T(128)}, f32[128,128]{1,0:T(8,128)S(1)}, f32[128,128]{1,0:T(8,128)S(1)}, s32[]{:T(128)}, s32[]{:T(128)}, /*index=5*/s32[]{:T(128)}) %tuple.231), condition=%wide.region_11.12_spmd.clone, body=%wide.region_10.11_spmd.clone.sunk | while | flops 197123 | bytes 69221 | solution.py:52
  1408.7 68.5 %all-reduce.13.cloned.1.call-done = f32[128,128]{1,0:T(8,128)} async-done(((f32[128,128]{1,0:T(8,128)}), f32[128,128]{1,0:T(8,128)}) %all-reduce.13.cloned.1.call-update) | async-done | bytes 65552 | tf_op jit(solution)/shard_map/psum | solution.py:76
  1478.1 257.4 %while.118 = (s32[]{:T(128)}, f32[128,128]{1,0:T(8,128)S(1)}, f32[128,128]{0,1:T(8,128)S(1)}, s32[]{:T(128)}, s32[]{:T(128)}) while((s32[]{:T(128)}, f32[128,128]{1,0:T(8,128)S(1)}, f32[128,128]{0,1:T(8,128)S(1)}, s32[]{:T(128)}, s32[]{:T(128)}) %tuple.234), condition=%wide.region_14.15_spmd.clone, body=%wide.region_13.14_spmd.clone.sunk | while | flops 197122 | bytes 71261 | solution.py:39
  1735.5 184.3 %while.119 = (s32[]{:T(128)}, f32[128,128]{1,0:T(8,128)S(1)}, f32[128,128]{1,0:T(8,128)S(1)}, s32[]{:T(128)}, s32[]{:T(128)}, /*index=5*/s32[]{:T(128)}) while((s32[]{:T(128)}, f32[128,128]{1,0:T(8,128)S(1)}, f32[128,128]{1,0:T(8,128)S(1)}, s32[]{:T(128)}, s32[]{:T(128)}, /*index=5*/s32[]{:T(128)}) %tuple.237), condition=%wide.region_16.17_spmd.clone, body=%wide.region_15.16_spmd.clone.sunk | while | flops 197123 | bytes 69221 | solution.py:52
  1920.8 31.4 %all-reduce.15.cloned.1.call-done = f32[256,128]{1,0:T(8,128)} async-done(((f32[256,128]{1,0:T(8,128)}), f32[256,128]{1,0:T(8,128)}) %all-reduce.15.cloned.1.call-update) | async-done | bytes 131088 | tf_op jit(solution)/shard_map/psum | solution.py:16
  1952.2 2.1 fusion.59
  1954.4 72.3 %all-reduce.17.cloned.1.call-done = f32[128,512]{1,0:T(8,128)} async-done(((f32[128,512]{1,0:T(8,128)}), f32[128,512]{1,0:T(8,128)}) %all-reduce.17.cloned.1.call-update) | async-done | bytes 262160 | tf_op jit(solution)/shard_map/psum | solution.py:103
  2026.8 2.4 fusion.43
  (3667 shorter events, 1478.4 us)
Async XLA Ops:
  7.2 78.1 %all-reduce.9.cloned.1.call-start = ((), (), s32[]{:S(2)}) async-start(), calls=%async_computation | async-start | bytes 524288 | tf_op jit(solution)/shard_map/psum | solution.py:92
  10.9 0.7 copy-start.4
  11.6 0.7 copy-start.5
  14.0 0.7 copy-start.6
  14.8 1.0 copy-start
  85.2 199.3 %all-reduce.19.cloned.1.call-start = ((), (), s32[]{:S(2)}) async-start(), calls=%async_computation.5 | async-start | bytes 524288 | tf_op jit(solution)/shard_map/while/body/eval_jaxpr/psum | solution.py:96
  286.5 199.4 %all-reduce.19.cloned.1.call-start = ((), (), s32[]{:S(2)}) async-start(), calls=%async_computation.5 | async-start | bytes 524288 | tf_op jit(solution)/shard_map/while/body/eval_jaxpr/psum | solution.py:96
  487.9 199.4 %all-reduce.19.cloned.1.call-start = ((), (), s32[]{:S(2)}) async-start(), calls=%async_computation.5 | async-start | bytes 524288 | tf_op jit(solution)/shard_map/while/body/eval_jaxpr/psum | solution.py:96
  689.2 199.4 %all-reduce.19.cloned.1.call-start = ((), (), s32[]{:S(2)}) async-start(), calls=%async_computation.5 | async-start | bytes 524288 | tf_op jit(solution)/shard_map/while/body/eval_jaxpr/psum | solution.py:96
  890.6 72.7 %all-reduce.11.cloned.1.call-start = ((), (), s32[]{:S(2)}) async-start(), calls=%async_computation.1 | async-start | bytes 131072 | tf_op jit(solution)/shard_map/psum | solution.py:72
  891.7 585.5 %all-reduce.13.cloned.1.call-start = ((), (), s32[]{:S(2)}) async-start(), calls=%async_computation.2 | async-start | bytes 131072 | tf_op jit(solution)/shard_map/psum | solution.py:76
  963.3 2.2 copy-start.3
  1408.6 543.6 %all-reduce.15.cloned.1.call-start = ((), (), s32[]{:S(2)}) async-start(), calls=%async_computation.3 | async-start | bytes 262144 | tf_op jit(solution)/shard_map/psum | solution.py:16
  1920.8 106.0 %all-reduce.17.cloned.1.call-start = ((), (), s32[]{:S(2)}) async-start(), calls=%async_computation.4 | async-start | bytes 524288 | tf_op jit(solution)/shard_map/psum | solution.py:103
  1954.3 72.5 %copy-start.2 = (f32[256,128]{1,0:T(8,128)S(1)}, f32[256,128]{1,0:T(8,128)}, u32[]{:S(2)}) copy-start(f32[256,128]{1,0:T(8,128)} %all-reduce.15.cloned.1.call-done) | copy-start | bytes 393220
  2026.8 2.4 copy-start.1
Sparse Core Ops, SparseCore 0:
  11.9 73.2 all-reduce.8
  90.4 70.1 all-reduce.18
  291.7 70.0 all-reduce.18
  492.7 70.1 all-reduce.18
  694.1 70.1 all-reduce.18
  895.5 67.7 all-reduce.10
  1408.7 68.4 all-reduce.12
  1920.9 31.2 all-reduce.14
  1956.2 70.5 all-reduce.16
where the time goes:
time: 2060 us; the launch traced here: 2040 us
  local copies, waits for them, and re-layouts  805 us (39%)
  matrix products  693 us (34%)
  waiting for transfers between devices  313 us (15%)
  loops' own time  203 us (10%)
    dot_general x1035, matrix products, product(): jnp.dot(left, right, precision=PRECISE, preferred_element_type=jnp.float32)  682 us
    dynamic_slice x768, local copies, waits for them, and re-layouts, row_step(): pivot = lax.dynamic_index_in_dim(row_now, row, 0, keepdims=False)  484 us
    another operation x2, loops' own time, cholesky_lower(): return lax.fori_loop(0, gram.shape[0], column_step, jnp.zeros_like(gram))  185 us
    dynamic_slice x256, local copies, waits for them, and re-layouts, column_step(): lax.dynamic_index_in_dim(target, column, 0, keepdims=False)  163 us
    dynamic_update_slice x256, local copies, waits for them, and re-layouts, column_step(): lax.dynamic_update_slice_in_dim(lower, new_column[:, None], column, 1)  91.8 us
    psum x1, waiting for transfers between devices, on_device(): tail_rows = lax.psum(transposed_product(basis_cols, work_block), 'row')  72.3 us
    psum x1, waiting for transfers between devices, orthonormalize(): gram_one = lax.psum(transposed_product(panel_cols, panel_cols), 'row')  71.6 us
    psum x1, waiting for transfers between devices, on_device(): gram_blocks = lax.psum(gram_blocks, 'row')  69.3 us
  transfers between devices with their start and end apart: 9, of which 5 were waited for; matrix products, arithmetic and copies ran while one was open for 38% of the time, Pallas kernels for 0%

commit v1 on v0

v1 whole, which is shorter than its diff:
```python
import functools

import jax
import jax.numpy as jnp
from jax import lax
from jax.experimental import pallas as pl
from jax.experimental.pallas import tpu as pltpu
from jax.sharding import PartitionSpec as P

PANEL = 128
STRIPS = 4
SHIFT_RATE = 1e-06
PRECISE = lax.Precision.HIGHEST
BLOCK = 256
STEP = 16


def mm(left, right):
    return jnp.dot(left, right, precision=PRECISE, preferred_element_type=jnp.float32)


def mm_t(left, right):
    return lax.dot_general(
        left, right, (((0,), (0,)), ((), ())), precision=PRECISE, preferred_element_type=jnp.float32
    )


def mm_nt(left, right):
    return lax.dot_general(
        left, right, (((1,), (1,)), ((), ())), precision=PRECISE, preferred_element_type=jnp.float32
    )


def cos_pi(turns):
    whole = jnp.round(turns)
    part = turns - whole
    odd = whole - 2.0 * jnp.floor(whole * 0.5)
    sign = 1.0 - 2.0 * odd
    sq = part * part
    coeffs = (
        -2.58068913900140e-02, 2.35330630358893e-01, -1.33526276885459e00,
        4.05871212641677e00, -4.93480220054468e00, 1.0,
    )
    acc = jnp.full_like(sq, 1.92957430940392e-03)
    for coeff in coeffs:
        acc = acc * sq + coeff
    return acc * sign


def factor_and_invert(gram, work):
    rows = lax.broadcasted_iota(jnp.int32, (PANEL, PANEL), 0)
    cols = lax.broadcasted_iota(jnp.int32, (PANEL, PANEL), 1)
    work[:, :PANEL] = gram
    work[:, PANEL:] = jnp.where(rows == cols, 1.0, 0.0)
    row_id = lax.broadcasted_iota(jnp.int32, (STEP, PANEL), 0)
    for block in range(PANEL // STEP):
        lo = block * STEP
        left = work[lo:lo + STEP, :PANEL]
        right = work[lo:lo + STEP, PANEL:]
        spread = [
            jnp.broadcast_to(left[:, lo + e:lo + e + 1], (STEP, PANEL)) for e in range(STEP)
        ]
        for c in range(STEP):
            pivot = spread[c][c:c + 1, :]
            scale = lax.rsqrt(pivot)
            scale = scale * (1.5 - 0.5 * pivot * scale * scale)
            mult = jnp.where(row_id > c, spread[c] * scale, 0.0)
            row_left = left[c:c + 1, :] * scale
            row_right = right[c:c + 1, :] * scale
            left = jnp.where(row_id == c, row_left, left - mult * row_left)
            right = jnp.where(row_id == c, row_right, right - mult * row_right)
            for e in range(c + 1, STEP):
                spread[e] = spread[e] - mult * (spread[e][c:c + 1, :] * scale)
        work[lo:lo + STEP, :PANEL] = left
        work[lo:lo + STEP, PANEL:] = right
        if lo + STEP < PANEL:
            both = jnp.concatenate([left, right], axis=1)
            update = mm_t(left, both)
            work[lo + STEP:, :] = work[lo + STEP:, :] - update[lo + STEP:, :]


def panel_kernel(points_ref, modes_ref, panel_ref, x_ref, upper_ref, base, work, gram):
    rows = points_ref.shape[1]
    width = modes_ref.shape[1]
    blocks = rows // BLOCK
    norm = float(rows) ** 0.5
    first = lax.axis_index("col") == 0
    lane = lax.broadcasted_iota(jnp.int32, (8, PANEL), 1)
    sub = lax.broadcasted_iota(jnp.int32, (8, PANEL), 0)
    pick_weight = jnp.where(sub == 3, 1.0, 0.0) + 0.0 * lane

    gram[...] = jnp.zeros_like(gram)

    @pl.loop(0, blocks)
    def _(b):
        at = pl.ds(pl.multiple_of(b * BLOCK, BLOCK), BLOCK)
        pts = points_ref[:, at]
        weight = mm_t(pts, pick_weight)
        cols = cos_pi(mm_t(pts, panel_ref[...])) * weight
        base[at, :] = cols
        gram[...] += mm_t(cols, cols)
        for q in range(width // PANEL):
            span = slice(q * PANEL, (q + 1) * PANEL)
            x_ref[at, span] = cos_pi(mm_t(pts, modes_ref[:, span])) * weight

    ri = lax.broadcasted_iota(jnp.int32, (PANEL, PANEL), 0)
    ci = lax.broadcasted_iota(jnp.int32, (PANEL, PANEL), 1)
    total = gram[...]
    trace = jnp.sum(jnp.where(ri == ci, total, 0.0))
    factor_and_invert(total + jnp.where(ri == ci, SHIFT_RATE * trace, 0.0), work)
    upper_one = jnp.where(ri <= ci, work[:, :PANEL], 0.0)
    gram[...] = jnp.zeros_like(gram)

    @pl.loop(0, blocks)
    def _(b):
        at = pl.ds(pl.multiple_of(b * BLOCK, BLOCK), BLOCK)
        cols = mm_nt(base[at, :], work[:, PANEL:])
        base[at, :] = cols
        gram[...] += mm_t(cols, cols)

    upper_ref[:, :PANEL] = upper_one
    factor_and_invert(gram[...], work)
    upper_one = upper_ref[:, :PANEL]
    upper_ref[...] = jnp.zeros_like(upper_ref)

    @pl.loop(0, blocks)
    def _(b):
        at = pl.ds(pl.multiple_of(b * BLOCK, BLOCK), BLOCK)
        cols = mm_nt(base[at, :], work[:, PANEL:])
        base[at, :] = cols
        upper_ref[...] += mm_t(cols, x_ref[at, :])

    @pl.loop(0, blocks)
    def _(b):
        at = pl.ds(pl.multiple_of(b * BLOCK, BLOCK), BLOCK)
        cols = base[at, :]
        rest = x_ref[at, :] - mm(cols, upper_ref[...])
        x_ref[at, :PANEL] = jnp.where(first, cols * norm, rest[:, :PANEL])
        x_ref[at, PANEL:] = rest[:, PANEL:]

    upper_ref[...] = upper_ref[...] / norm
    upper_ref[:, :PANEL] = jnp.where(first, upper_one / norm, upper_ref[:, :PANEL])


def reflect_kernel(v_ref, x_ref, out_ref, gram, coeffs):
    rows, depth = v_ref.shape
    blocks = rows // BLOCK
    own_rows = out_ref.shape[0]
    panels = depth // PANEL
    gram[...] = jnp.zeros_like(gram)
    coeffs[...] = jnp.zeros_like(coeffs)

    @pl.loop(0, blocks)
    def _(b):
        at = pl.ds(pl.multiple_of(b * BLOCK, BLOCK), BLOCK)
        for k in range(panels):
            cut = slice(k * PANEL, (k + 1) * PANEL)
            part = v_ref[at, cut]
            upto = slice(0, (k + 1) * PANEL)
            gram[cut, upto] += mm_t(part, v_ref[at, upto])
            coeffs[cut, :] += mm_t(part, x_ref[at, :])

    ri = lax.broadcasted_iota(jnp.int32, (PANEL, PANEL), 0)
    ci = lax.broadcasted_iota(jnp.int32, (PANEL, PANEL), 1)
    blocks_t = []
    inverses = []
    for k in range(panels):
        cut = slice(k * PANEL, (k + 1) * PANEL)
        tri = gram[cut, cut]
        half = jnp.sum(jnp.where(ri == ci, 0.5 * tri, 0.0), axis=0, keepdims=True)
        blocks_t.append(tri)
        inverses.append(jnp.where(ri == ci, 1.0 / half, 0.0))
    size = 1
    while size < PANEL:
        mask = (
            (ri // (2 * size) == ci // (2 * size))
            & ((ri // size) % 2 == 1)
            & ((ci // size) % 2 == 0)
        )
        halfway = [mm(jnp.where(mask, t, 0.0), inv) for t, inv in zip(blocks_t, inverses)]
        inverses = [inv - mm(inv, h) for h, inv in zip(halfway, inverses)]
        size *= 2
    for k in range(panels):
        cut = slice(k * PANEL, (k + 1) * PANEL)
        right = coeffs[cut, :]
        if k:
            right = right - mm(gram[cut, :k * PANEL], coeffs[:k * PANEL, :])
        coeffs[cut, :] = mm(inverses[k], right)
    own = pl.ds(pl.multiple_of(lax.axis_index("row") * own_rows, own_rows), own_rows)
    out_ref[...] = x_ref[own, :] - mm(v_ref[own, :], coeffs[...])


def on_device(points, strip_ids, counts, mode_index, reflectors):
    own_rows = points.shape[1]
    width = 2 * mode_index.shape[0]
    rows = own_rows * lax.axis_size("row")
    depth = reflectors.shape[1]
    live = (jnp.arange(own_rows, dtype=jnp.int32) < counts[0]).astype(jnp.float32)
    stored = lax.all_gather(reflectors * live[:, None], "row", axis=0, tiled=True)
    weight = 3.0 * jnp.power(10.0, -strip_ids.astype(jnp.float32) / (STRIPS - 1)) * live
    one = jnp.ones((own_rows,), jnp.float32)
    zero = jnp.zeros((own_rows,), jnp.float32)
    pts = jnp.stack([points[0], points[1], one, weight, zero, zero, zero, zero])
    pts = lax.all_gather(pts, "row", axis=1, tiled=True)
    modes = jnp.repeat(mode_index, 2)
    column = jnp.arange(width, dtype=jnp.int32)
    blank = jnp.zeros((width,), jnp.float32)
    table = jnp.stack([
        (modes // 128 - 128).astype(jnp.float32),
        (modes % 128 + 1).astype(jnp.float32),
        -0.5 * (column % 2).astype(jnp.float32),
        blank, blank, blank, blank, blank,
    ])
    panel = lax.all_gather(table[:, :PANEL], "col", axis=0, tiled=True)[:8]
    vmem = pl.BlockSpec(memory_space=pltpu.VMEM)
    x, upper = pl.pallas_call(
        panel_kernel,
        out_shape=(
            jax.ShapeDtypeStruct((rows, width), jnp.float32),
            jax.ShapeDtypeStruct((PANEL, width), jnp.float32),
        ),
        in_specs=[vmem] * 3,
        out_specs=(vmem, vmem),
        scratch_shapes=[
            pltpu.VMEM((rows, PANEL), jnp.float32),
            pltpu.VMEM((PANEL, 2 * PANEL), jnp.float32),
            pltpu.VMEM((PANEL, PANEL), jnp.float32),
        ],
        compiler_params=pltpu.CompilerParams(vmem_limit_bytes=40 * 2**20),
        name="panel",
    )(pts, table, panel)
    out = pl.pallas_call(
        reflect_kernel,
        out_shape=jax.ShapeDtypeStruct((own_rows, width), jnp.float32),
        in_specs=[vmem] * 2,
        out_specs=vmem,
        scratch_shapes=[
            pltpu.VMEM((depth, depth), jnp.float32),
            pltpu.VMEM((depth, width), jnp.float32),
        ],
        compiler_params=pltpu.CompilerParams(vmem_limit_bytes=40 * 2**20),
        name="reflect",
    )(stored, x)
    return (out, upper)


def solution(mesh):
    return jax.shard_map(
        on_device,
        mesh=mesh,
        in_specs=(P(None, "row"), P("row"), P("row"), P("col"), P("row", None)),
        out_specs=(P("row", "col"), P(None, "col")),
        check_vma=False,
    )
```

time: 2060 us -> 125 us (0.06); the launches traced: 2040 us -> 124 us
  local copies, waits for them, and re-layouts: 805 us -> 7.47 us
  matrix products: 693 us -> 0 us
  waiting for transfers between devices: 313 us -> 0.02 us
  loops' own time: 203 us -> 0 us
  Pallas kernels: 0 us -> 60.8 us
  blocking collectives: 0 us -> 37.8 us
    dot_general x1043 -> x0, matrix products: 693 us -> none  [the longest x1035 682 us: product(): jnp.dot(left, right, precision=PRECISE, preferred_element_type=jnp.float32)]
    dynamic_slice x1032 -> x0, local copies, waits for them, and re-layouts: 651 us -> none  [the longest x768 484 us: row_step(): pivot = lax.dynamic_index_in_dim(row_now, row, 0, keepdims=False)]
    psum x9 -> x0, waiting for transfers between devices: 313 us -> none  [the longest x1 72.3 us: on_device(): tail_rows = lax.psum(transposed_product(basis_cols, work_block), 'row')]
    another operation x9 -> x0, loops' own time: 203 us -> none  [the longest x2 185 us: cholesky_lower(): return lax.fori_loop(0, gram.shape[0], column_step, jnp.zeros_like(gram))]
    dynamic_update_slice x1024 -> x0, local copies, waits for them, and re-layouts: 116 us -> none  [the longest x256 91.8 us: column_step(): lax.dynamic_update_slice_in_dim(lower, new_column[:, None], column, 1)]
    pallas_call x0 -> x2, Pallas kernels: none -> 60.8 us  [the longest x1 38.1 us: on_device(): pl.pallas_call(panel_kernel, out_shape=(jax.ShapeDtypeStruct((rows, width...]
    all_gather x0 -> x2, blocking collectives: none -> 37.8 us  [the longest x1 31.6 us: on_device(): pts = lax.all_gather(pts, 'row', axis=1, tiled=True)]
    broadcast_in_dim x256 -> x1, local copies, waits for them, and re-layouts: 29 us -> 0.77 us  [on_device(): modes = jnp.repeat(mode_index, 2)]
  transfers between devices with their start and end apart: 9 -> 1, of which waited for: 5 -> 0; matrix products, arithmetic and copies ran while one was open for 38% -> 2% of each run, Pallas kernels for 0% -> 31%
where the time goes in v1:
time: 125 us; the launch traced here: 124 us
  Pallas kernels  60.8 us (49%)
  blocking collectives  37.8 us (30%)
  between operations  14.7 us (12%)
  local copies, waits for them, and re-layouts  7.47 us (6%)
  other arithmetic  3.42 us (3%)
    pallas_call x1, Pallas kernels, on_device(): pl.pallas_call(panel_kernel, out_shape=(jax.ShapeDtypeStruct((rows, width...  38.1 us
    all_gather x1, blocking collectives, on_device(): pts = lax.all_gather(pts, 'row', axis=1, tiled=True)  31.6 us
    pallas_call x1, Pallas kernels, on_device(): pl.pallas_call(reflect_kernel, out_shape=jax.ShapeDtypeStruct((own_rows,...  22.7 us
    unnamed x6, local copies, waits for them, and re-layouts  6.36 us
    all_gather x1, blocking collectives, on_device(): panel = lax.all_gather(table[:, :PANEL], 'col', axis=0, tiled=True)[:8]  6.22 us
  transfers between devices with their start and end apart: 1, of which 0 were waited for; matrix products, arithmetic and copies ran while one was open for 2% of the time, Pallas kernels for 31%

profile of v1, /device:TPU:0, one launch (start us, length us, event | category | flops | bytes accessed | tf_op | source)
XLA Modules:
  0.0 124.3 jit_solution(10712059693491768966)
XLA Ops:
  7.2 0.0 all-gather.2.cloned.1.call-start
  7.9 1.9 %broadcast_multiply_fusion = f32[256,512]{1,0:T(8,128)} fusion(f32[256,512]{1,0:T(8,128)} %param.9, f32[256]{0:T(256)S(1)} %fusion.4), kind=kLoop, calls=%fused_computation | loop fusion | flops 131072 | bytes 1049600 | tf_op jit(solution)/shard_map/mul | solution.py:199
  9.8 0.0 all-gather.2.cloned.1.call-update
  9.8 0.1 pad.1.clone
  9.9 0.1 pad.3.clone
  10.0 0.8 broadcast_in_dim.4
  10.8 0.1 reshape.154
  11.0 6.2 %all_gather.11 = f32[32,128]{1,0:T(8,128)S(1)} all-gather(f32[8,128]{1,0:T(8,128)S(1)} %slice.11), channel_id=1, replica_groups=mesh['row'=8,'col'=4] {'col'}, dimensions={0}, use_global_device_ids=true | all-gather | bytes 20480 | tf_op jit(solution)/shard_map/all_gather | solution.py:214
  17.2 0.7 multiply_select_fusion
  17.9 0.8 maximum_maximum_fusion
  18.7 31.6 %all_gather.10.points_ref = f32[8,2048]{1,0:T(8,128)S(1)} all-gather(f32[8,256]{1,0:T(8,128)S(1)} %maximum_maximum_fusion), channel_id=1, replica_groups=mesh['row'=8,'col'=4] {'row'}, dimensions={1}, use_global_device_ids=true | all-gather | bytes 73728 | tf_op jit(solution)/shard_map/all_gather | solution.py:204
  50.3 38.1 %panel.1 = (f32[2048,512]{1,0:T(8,128)S(1)}, f32[128,512]{1,0:T(8,128)}) custom-call(f32[8,2048]{1,0:T(8,128)S(1)} %all_gather.10.points_ref, f32[8,512]{1,0:T(8,128)S(1)} %stack.23.modes_ref, f32[8,128]{1,0:T(8,128)S(1)} %slice.12.panel_ref), custom_call_target="tpu_custom_call" | custom-call | tf_op jit(solution)/shard_map/panel/pallas_call | solution.py:216
  88.4 0.0 copy-start.1
  88.4 2.0 %copy-done.1 = f32[2048,512]{1,0:T(8,128)} copy-done((f32[2048,512]{1,0:T(8,128)}, f32[2048,512]{1,0:T(8,128)S(1)}, u32[]{:S(2)}) %copy-start.1) | copy-done | bytes 4194328
  90.3 0.0 all-gather.2.cloned.1.call-done.v_ref
  90.3 0.0 copy-start
  90.4 2.2 %copy-done = f32[2048,512]{1,0:T(8,128)S(1)} copy-done((f32[2048,512]{1,0:T(8,128)S(1)}, f32[2048,512]{1,0:T(8,128)}, u32[]{:S(2)}) %copy-start) | copy-done | bytes 4194328
  92.5 0.0 copy-start.2
  92.5 2.2 %copy-done.2 = f32[2048,512]{1,0:T(8,128)S(1)} copy-done((f32[2048,512]{1,0:T(8,128)S(1)}, f32[2048,512]{1,0:T(8,128)}, u32[]{:S(2)}) %copy-start.2) | copy-done | bytes 4194328
  94.7 22.7 %reflect.1 = f32[256,512]{1,0:T(8,128)} custom-call(f32[2048,512]{1,0:T(8,128)S(1)} %copy-done, f32[2048,512]{1,0:T(8,128)S(1)} %copy-done.2), custom_call_target="tpu_custom_call" | custom-call | tf_op jit(solution)/shard_map/reflect/pallas_call | solution.py:232
  (10 shorter events, 0.1 us)
Async XLA Ops:
  7.2 83.2 %all-gather.2.cloned.1.call-start = ((), (), s32[]{:S(2)}) async-start(), calls=%async_computation | async-start | bytes 4718592 | tf_op jit(solution)/shard_map/all_gather | solution.py:199
  88.4 2.0 %copy-start.1 = (f32[2048,512]{1,0:T(8,128)}, f32[2048,512]{1,0:T(8,128)S(1)}, u32[]{:S(2)}) copy-start(f32[2048,512]{1,0:T(8,128)S(1)} %get-tuple-element.4.x_ref) | copy-start | bytes 12582916
  90.3 2.2 %copy-start = (f32[2048,512]{1,0:T(8,128)S(1)}, f32[2048,512]{1,0:T(8,128)}, u32[]{:S(2)}) copy-start(f32[2048,512]{1,0:T(8,128)} %all-gather.2.cloned.1.call-done.v_ref) | copy-start | bytes 12582916
  92.5 2.2 %copy-start.2 = (f32[2048,512]{1,0:T(8,128)S(1)}, f32[2048,512]{1,0:T(8,128)}, u32[]{:S(2)}) copy-start(f32[2048,512]{1,0:T(8,128)} %copy-done.1) | copy-start | bytes 12582916
Sparse Core Ops, SparseCore 0:
  10.7 76.5 all-gather.1

commit v2 on v1

v2 whole, which is shorter than its diff:
```python
import functools

import jax
import jax.numpy as jnp
from jax import lax
from jax.experimental import pallas as pl
from jax.experimental.pallas import tpu as pltpu
from jax.sharding import PartitionSpec as P

PANEL = 128
STRIPS = 4
SHIFT_RATE = 1e-06
PRECISE = lax.Precision.HIGHEST
STEP = 16


def mm(left, right):
    return jnp.dot(left, right, precision=PRECISE, preferred_element_type=jnp.float32)


def mm_t(left, right):
    return lax.dot_general(
        left, right, (((0,), (0,)), ((), ())), precision=PRECISE, preferred_element_type=jnp.float32
    )


def mm_nt(left, right):
    return lax.dot_general(
        left, right, (((1,), (1,)), ((), ())), precision=PRECISE, preferred_element_type=jnp.float32
    )


def cos_pi(turns):
    whole = jnp.round(turns)
    part = turns - whole
    odd = whole - 2.0 * jnp.floor(whole * 0.5)
    sign = 1.0 - 2.0 * odd
    sq = part * part
    coeffs = (
        -2.58068913900140e-02, 2.35330630358893e-01, -1.33526276885459e00,
        4.05871212641677e00, -4.93480220054468e00, 1.0,
    )
    acc = jnp.full_like(sq, 1.92957430940392e-03)
    for coeff in coeffs:
        acc = acc * sq + coeff
    return acc * sign


def factor_and_invert(gram, work, between=None):
    rows = lax.broadcasted_iota(jnp.int32, (PANEL, PANEL), 0)
    cols = lax.broadcasted_iota(jnp.int32, (PANEL, PANEL), 1)
    work[:, :PANEL] = gram
    work[:, PANEL:] = jnp.where(rows == cols, 1.0, 0.0)
    row_id = lax.broadcasted_iota(jnp.int32, (STEP, PANEL), 0)
    for block in range(PANEL // STEP):
        lo = block * STEP
        if between is not None:
            between(block)
        left = work[lo:lo + STEP, :PANEL]
        right = work[lo:lo + STEP, PANEL:]
        spread = [
            jnp.broadcast_to(left[:, lo + e:lo + e + 1], (STEP, PANEL)) for e in range(STEP)
        ]
        for c in range(STEP):
            pivot = spread[c][c:c + 1, :]
            scale = lax.rsqrt(pivot)
            scale = scale * (1.5 - 0.5 * pivot * scale * scale)
            mult = jnp.where(row_id > c, spread[c] * scale, 0.0)
            row_left = left[c:c + 1, :] * scale
            row_right = right[c:c + 1, :] * scale
            left = jnp.where(row_id == c, row_left, left - mult * row_left)
            right = jnp.where(row_id == c, row_right, right - mult * row_right)
            for e in range(c + 1, STEP):
                spread[e] = spread[e] - mult * (spread[e][c:c + 1, :] * scale)
        work[lo:lo + STEP, :PANEL] = left
        work[lo:lo + STEP, PANEL:] = right
        if lo + STEP < PANEL:
            both = jnp.concatenate([left, right], axis=1)
            update = mm_t(left, both)
            work[lo + STEP:, :] = work[lo + STEP:, :] - update[lo + STEP:, :]


def kernel(
    n_row, n_col, pts_in, modes_ref, v_in, out_ref, upper_ref,
    pts_all, panel_all, v_all, x_all, base, work, gram, big_gram, coeffs,
    pts_send, pts_recv, panel_send, panel_recv,
    push_send, push_recv, side_send, side_recv, core_send, core_recv,
):
    own_rows, depth = v_in.shape
    width = modes_ref.shape[1]
    panels = depth // PANEL
    rows = n_row * own_rows
    norm = float(rows) ** 0.5
    me = lax.axis_index("row")
    col = lax.axis_index("col")
    n_side = n_col // 2
    side = col // 2
    core = col % 2
    first = col == 0
    piece = own_rows // n_col

    def row_peer(k):
        return (lax.rem(me + k, n_row), col)

    def col_peer(k):
        return (me, lax.rem(col + k, n_col))

    def side_peer(k):
        return (me, lax.rem(side + k, n_side) * 2 + core)

    core_peer = (me, side * 2 + 1 - core)

    def source(k):
        return lax.rem(me + n_row - k, n_row)

    def piece_at(row, core_id, side_id):
        at = row * own_rows + (core_id * n_side + side_id) * piece
        return pl.ds(pl.multiple_of(at, piece), piece)

    def half_at(row, core_id):
        at = row * own_rows + core_id * n_side * piece
        return pl.ds(pl.multiple_of(at, piece), n_side * piece)

    def remote(src, dst, send, recv, peer):
        return pltpu.make_async_remote_copy(
            src_ref=src, dst_ref=dst, send_sem=send, recv_sem=recv,
            device_id=peer, device_id_type=pl.DeviceIdType.MESH,
        )

    def pts_copy(k, row):
        return remote(pts_in, pts_all.at[row], pts_send.at[k], pts_recv.at[k], row_peer(k))

    def panel_copy(k, index):
        return remote(
            modes_ref.at[:, pl.ds(0, PANEL)], panel_all.at[index],
            panel_send.at[k], panel_recv.at[k], col_peer(k),
        )

    def push_copy(k, row):
        mine = (core * n_side + side) * piece
        return remote(
            v_in.at[pl.ds(pl.multiple_of(mine, piece), piece)], v_all.at[piece_at(row, core, side)],
            push_send.at[k], push_recv.at[k], row_peer(k),
        )

    def side_copy(k, j, side_id):
        at = v_all.at[piece_at(source(k), core, side_id)]
        return remote(at, at, side_send.at[k, j], side_recv.at[k, j], side_peer(j))

    def core_copy(k, core_id):
        at = v_all.at[half_at(source(k), core_id)]
        return remote(at, at, core_send.at[k], core_recv.at[k], core_peer)

    barrier = pltpu.get_barrier_semaphore()
    for k in range(1, n_row):
        pl.semaphore_signal(barrier, inc=1, device_id=row_peer(k), device_id_type=pl.DeviceIdType.MESH)
    for k in range(1, n_col):
        pl.semaphore_signal(barrier, inc=1, device_id=col_peer(k), device_id_type=pl.DeviceIdType.MESH)
    pl.semaphore_wait(barrier, n_row + n_col - 2)

    for k in range(1, n_col):
        panel_copy(k, col).start()
    for k in range(1, n_row):
        pts_copy(k, me).start()
    for k in range(1, n_row):
        push_copy(k, me).start()
    pts_all[me] = pts_in[...]
    panel_all[col] = modes_ref[:, :PANEL]
    v_all[pl.ds(pl.multiple_of(me * own_rows, own_rows), own_rows), :] = v_in[...]
    for k in range(1, n_col):
        panel_copy(k, lax.rem(col + n_col - k, n_col)).wait_recv()
    for k in range(1, n_row):
        pts_copy(k, source(k)).wait_recv()

    def forward_sides(ks):
        for k in ks:
            push_copy(k, source(k)).wait_recv()
            for j in range(1, n_side):
                side_copy(k, j, side).start()

    def forward_core(ks):
        for k in ks:
            for j in range(1, n_side):
                side_copy(k, j, lax.rem(side + n_side - j, n_side)).wait_recv()
            core_copy(k, core).start()

    slots = PANEL // STEP
    share = -(-(n_row - 1) // slots)

    def turn(action):
        return lambda b: action(range(1 + b * share, min(n_row, 1 + (b + 1) * share)))

    lane = lax.broadcasted_iota(jnp.int32, (8, PANEL), 1)
    sub = lax.broadcasted_iota(jnp.int32, (8, PANEL), 0)
    pick_weight = jnp.where(sub == 3, 1.0, 0.0) + 0.0 * lane
    pick_live = jnp.where(sub == 4, 1.0, 0.0) + 0.0 * lane

    def rows_of(b):
        return pl.ds(pl.multiple_of(b * own_rows, own_rows), own_rows)

    gram[...] = jnp.zeros_like(gram)

    @pl.loop(0, n_row)
    def _(b):
        at = rows_of(b)
        pts = pts_all[b]
        weight = mm_t(pts, pick_weight)
        cols = cos_pi(mm_t(pts, panel_all[0])) * weight
        base[at, :] = cols
        gram[...] += mm_t(cols, cols)
        for q in range(width // PANEL):
            span = slice(q * PANEL, (q + 1) * PANEL)
            x_all[at, span] = cos_pi(mm_t(pts, modes_ref[:, span])) * weight

    ri = lax.broadcasted_iota(jnp.int32, (PANEL, PANEL), 0)
    ci = lax.broadcasted_iota(jnp.int32, (PANEL, PANEL), 1)
    total = gram[...]
    trace = jnp.sum(jnp.where(ri == ci, total, 0.0))
    factor_and_invert(
        total + jnp.where(ri == ci, SHIFT_RATE * trace, 0.0), work, turn(forward_sides)
    )
    upper_ref[:, :PANEL] = jnp.where(ri <= ci, work[:, :PANEL], 0.0)
    gram[...] = jnp.zeros_like(gram)

    @pl.loop(0, n_row)
    def _(b):
        at = rows_of(b)
        cols = mm_nt(base[at, :], work[:, PANEL:])
        base[at, :] = cols
        gram[...] += mm_t(cols, cols)

    factor_and_invert(gram[...], work, turn(forward_core))
    upper_one = upper_ref[:, :PANEL]
    upper_ref[...] = jnp.zeros_like(upper_ref)

    @pl.loop(0, n_row)
    def _(b):
        at = rows_of(b)
        cols = mm_nt(base[at, :], work[:, PANEL:])
        base[at, :] = cols
        upper_ref[...] += mm_t(cols, x_all[at, :])

    for k in range(1, n_row):
        core_copy(k, 1 - core).wait_recv()

    big_gram[...] = jnp.zeros_like(big_gram)
    coeffs[...] = jnp.zeros_like(coeffs)

    @pl.loop(0, n_row)
    def _(b):
        at = rows_of(b)
        cols = base[at, :]
        rest = x_all[at, :] - mm(cols, upper_ref[...])
        x_all[at, :PANEL] = jnp.where(first, cols * norm, rest[:, :PANEL])
        x_all[at, PANEL:] = rest[:, PANEL:]
        live = mm_t(pts_all[b], pick_live)
        for k in range(panels):
            cut = slice(k * PANEL, (k + 1) * PANEL)
            upto = slice(0, (k + 1) * PANEL)
            big_gram[cut, upto] += mm_t(v_all[at, cut] * live, v_all[at, upto])

    def coefficients(b):
        at = rows_of(b)
        coeffs[...] += mm_t(v_all[at, :], x_all[at, :])

    blocks_t = []
    inverses = []
    for k in range(panels):
        cut = slice(k * PANEL, (k + 1) * PANEL)
        tri = big_gram[cut, cut]
        half = jnp.sum(jnp.where(ri == ci, 0.5 * tri, 0.0), axis=0, keepdims=True)
        blocks_t.append(tri)
        inverses.append(jnp.where(ri == ci, 1.0 / half, 0.0))
    size = 1
    done = 0
    while size < PANEL:
        mask = (
            (ri // (2 * size) == ci // (2 * size))
            & ((ri // size) % 2 == 1)
            & ((ci // size) % 2 == 0)
        )
        if done < n_row:
            coefficients(done)
            done += 1
        halfway = [mm(jnp.where(mask, t, 0.0), inv) for t, inv in zip(blocks_t, inverses)]
        inverses = [inv - mm(inv, h) for h, inv in zip(halfway, inverses)]
        size *= 2

    @pl.loop(done, n_row)
    def _(b):
        coefficients(b)

    for k in range(panels):
        cut = slice(k * PANEL, (k + 1) * PANEL)
        right = coeffs[cut, :]
        if k:
            right = right - mm(big_gram[cut, :k * PANEL], coeffs[:k * PANEL, :])
        coeffs[cut, :] = mm(inverses[k], right)
    live = mm_t(pts_in[...], pick_live)
    shift = mm(v_in[...], coeffs[...])
    at = rows_of(me)
    for q in range(width // PANEL):
        span = slice(q * PANEL, (q + 1) * PANEL)
        out_ref[:, span] = x_all[at, span] - shift[:, span] * live
    upper_ref[...] = upper_ref[...] / norm
    upper_ref[:, :PANEL] = jnp.where(first, upper_one / norm, upper_ref[:, :PANEL])

    for k in range(1, n_col):
        panel_copy(k, col).wait_send()
    for k in range(1, n_row):
        pts_copy(k, me).wait_send()
        push_copy(k, me).wait_send()
        for j in range(1, n_side):
            side_copy(k, j, side).wait_send()
        core_copy(k, core).wait_send()


def on_device(points, strip_ids, counts, mode_index, reflectors):
    own_rows = points.shape[1]
    width = 2 * mode_index.shape[0]
    n_row = lax.axis_size("row")
    n_col = lax.axis_size("col")
    rows = own_rows * n_row
    depth = reflectors.shape[1]
    live = (jnp.arange(own_rows, dtype=jnp.int32) < counts[0]).astype(jnp.float32)
    weight = 3.0 * jnp.power(10.0, -strip_ids.astype(jnp.float32) / (STRIPS - 1)) * live
    one = jnp.ones((own_rows,), jnp.float32)
    zero = jnp.zeros((own_rows,), jnp.float32)
    pts = jnp.stack([points[0], points[1], one, weight, live, zero, zero, zero])
    modes = jnp.repeat(mode_index, 2)
    column = jnp.arange(width, dtype=jnp.int32)
    blank = jnp.zeros((width,), jnp.float32)
    table = jnp.stack([
        (modes // 128 - 128).astype(jnp.float32),
        (modes % 128 + 1).astype(jnp.float32),
        -0.5 * (column % 2).astype(jnp.float32),
        blank, blank, blank, blank, blank,
    ])
    vmem = pl.BlockSpec(memory_space=pltpu.VMEM)
    dma = pltpu.SemaphoreType.DMA
    n_side = n_col // 2
    return pl.pallas_call(
        functools.partial(kernel, n_row, n_col),
        out_shape=(
            jax.ShapeDtypeStruct((own_rows, width), jnp.float32),
            jax.ShapeDtypeStruct((PANEL, width), jnp.float32),
        ),
        in_specs=[vmem] * 3,
        out_specs=(vmem, vmem),
        scratch_shapes=[
            pltpu.VMEM((n_row, 8, own_rows), jnp.float32),
            pltpu.VMEM((n_col, 8, PANEL), jnp.float32),
            pltpu.VMEM((rows, depth), jnp.float32),
            pltpu.VMEM((rows, width), jnp.float32),
            pltpu.VMEM((rows, PANEL), jnp.float32),
            pltpu.VMEM((PANEL, 2 * PANEL), jnp.float32),
            pltpu.VMEM((PANEL, PANEL), jnp.float32),
            pltpu.VMEM((depth, depth), jnp.float32),
            pltpu.VMEM((depth, width), jnp.float32),
            dma((n_row,)), dma((n_row,)), dma((n_col,)), dma((n_col,)),
            dma((n_row,)), dma((n_row,)),
            dma((n_row, n_side)), dma((n_row, n_side)),
            dma((n_row,)), dma((n_row,)),
        ],
        compiler_params=pltpu.CompilerParams(
            vmem_limit_bytes=48 * 2**20, collective_id=0, has_side_effects=True
        ),
        name="window",
    )(pts, table, reflectors)


def solution(mesh):
    return jax.shard_map(
        on_device,
        mesh=mesh,
        in_specs=(P(None, "row"), P("row"), P("row"), P("col"), P("row", None)),
        out_specs=(P("row", "col"), P(None, "col")),
        check_vma=False,
    )
```

time: 125 us -> 91 us (0.73)
  the two profiles are of different devices: /device:TPU:0 before, /device:TPU:10 now
where the time goes in v2:
time: 91 us; the launch traced here: 90.8 us
  Pallas kernels  84.5 us (93%)
  local copies, waits for them, and re-layouts  4.82 us (5%)
  between operations  1.39 us (2%)
    pallas_call x1, Pallas kernels, on_device(): pl.pallas_call(functools.partial(kernel, n_row, n_col), out_shape=(jax.Sh...  84.5 us
    unnamed x10, local copies, waits for them, and re-layouts  4.52 us

profile of v2, /device:TPU:10, one launch (start us, length us, event | category | flops | bytes accessed | tf_op | source)
XLA Modules:
  0.0 90.8 jit_solution(16930411712641072478)
XLA Ops:
  1.3 0.0 copy-start.3
  1.3 0.7 copy-done.3
  2.0 0.0 copy-start.1
  2.0 0.7 copy-done.1
  2.7 0.0 copy-start.2
  2.7 0.7 copy-done.2
  3.4 0.1 broadcast_in_dim.3
  3.5 0.1 reshape.159
  3.7 0.0 copy-start
  3.7 1.0 %copy-done = f32[256,512]{1,0:T(8,128)S(1)} copy-done((f32[256,512]{1,0:T(8,128)S(1)}, f32[256,512]{1,0:T(8,128)}, u32[]{:S(2)}) %copy-start) | copy-done | bytes 524312
  4.8 84.5 %window.1 = (f32[256,512]{1,0:T(8,128)S(1)}, f32[128,512]{1,0:T(8,128)S(1)}) custom-call(f32[8,256]{1,0:T(8,128)S(1)} %stack.21.pts_in, f32[8,512]{1,0:T(8,128)S(1)} %stack.23.modes_ref, f32[256,512]{1,0:T(8,128)S(1)} %copy-done), custom_call_target="tpu_custom_call" | custom-call | tf_op jit(solution)/shard_map/window/pallas_call | solution.py:342
  89.3 0.8 copy.10
  90.1 0.7 copy.11
  (12 shorter events, 0.1 us)
Async XLA Ops:
  1.3 0.7 copy-start.3
  2.0 0.7 copy-start.1
  2.7 0.7 copy-start.2
  3.7 1.0 %copy-start = (f32[256,512]{1,0:T(8,128)S(1)}, f32[256,512]{1,0:T(8,128)}, u32[]{:S(2)}) copy-start(f32[256,512]{1,0:T(8,128)} %v_in.1) | copy-start | bytes 1572868

commit v3 on v2

--- a/solution.py
+++ b/solution.py
@@ -22,6 +22,29 @@
     return lax.dot_general(
         left, right, (((0,), (0,)), ((), ())), precision=PRECISE, preferred_element_type=jnp.float32
     )
+
+
+def halves(value):
+    top = value.astype(jnp.bfloat16)
+    return top, (value - top.astype(jnp.float32)).astype(jnp.bfloat16)
+
+
+def three_products(left, right, dims):
+    left_top, left_rest = halves(left)
+    right_top, right_rest = halves(right)
+
+    def one(a, b):
+        return lax.dot_general(a, b, (dims, ((), ())), preferred_element_type=jnp.float32)
+
+    return one(left_rest, right_top) + one(left_top, right_rest) + one(left_top, right_top)
+
+
+def mm_high(left, right):
+    return three_products(left, right, ((1,), (0,)))
+
+
+def mm_t_high(left, right):
+    return three_products(left, right, ((0,), (0,)))
 
 
 def mm_nt(left, right):
@@ -99,8 +122,17 @@
     first = col == 0
     piece = own_rows // n_col
 
+    def flipped(k):
+        index = me
+        bit = 1
+        while bit < n_row:
+            if k & bit:
+                index = index + (1 - 2 * ((me // bit) % 2)) * bit
+            bit *= 2
+        return index
+
     def row_peer(k):
-        return (lax.rem(me + k, n_row), col)
+        return (flipped(k), col)
 
     def col_peer(k):
         return (me, lax.rem(col + k, n_col))
@@ -111,7 +143,7 @@
     core_peer = (me, side * 2 + 1 - core)
 
     def source(k):
-        return lax.rem(me + n_row - k, n_row)
+        return flipped(k)
 
     def piece_at(row, core_id, side_id):
         at = row * own_rows + (core_id * n_side + side_id) * piece
@@ -185,10 +217,19 @@
             core_copy(k, core).start()
 
     slots = PANEL // STEP
-    share = -(-(n_row - 1) // slots)
-
-    def turn(action):
-        return lambda b: action(range(1 + b * share, min(n_row, 1 + (b + 1) * share)))
+    near = list(range(1, n_row // 2))
+    far = list(range(n_row // 2, n_row))
+
+    def dealt(items, block, start):
+        span = slots - start
+        return [k for i, k in enumerate(items) if start + i * span // len(items) == block]
+
+    def during_first(block):
+        forward_sides(dealt(near, block, slots - 3))
+
+    def during_second(block):
+        forward_sides(dealt(far, block, 1))
+        forward_core(dealt(near, block, slots - 3))
 
     lane = lax.broadcasted_iota(jnp.int32, (8, PANEL), 1)
     sub = lax.broadcasted_iota(jnp.int32, (8, PANEL), 0)
@@ -217,7 +258,7 @@
     total = gram[...]
     trace = jnp.sum(jnp.where(ri == ci, total, 0.0))
     factor_and_invert(
-        total + jnp.where(ri == ci, SHIFT_RATE * trace, 0.0), work, turn(forward_sides)
+        total + jnp.where(ri == ci, SHIFT_RATE * trace, 0.0), work, during_first
     )
     upper_ref[:, :PANEL] = jnp.where(ri <= ci, work[:, :PANEL], 0.0)
     gram[...] = jnp.zeros_like(gram)
@@ -229,7 +270,7 @@
         base[at, :] = cols
         gram[...] += mm_t(cols, cols)
 
-    factor_and_invert(gram[...], work, turn(forward_core))
+    factor_and_invert(gram[...], work, during_second)
     upper_one = upper_ref[:, :PANEL]
     upper_ref[...] = jnp.zeros_like(upper_ref)
 
@@ -238,11 +279,9 @@
         at = rows_of(b)
         cols = mm_nt(base[at, :], work[:, PANEL:])
         base[at, :] = cols
-        upper_ref[...] += mm_t(cols, x_all[at, :])
-
-    for k in range(1, n_row):
-        core_copy(k, 1 - core).wait_recv()
-
+        upper_ref[...] += mm_t_high(cols, x_all[at, :])
+
+    forward_core(far)
     big_gram[...] = jnp.zeros_like(big_gram)
     coeffs[...] = jnp.zeros_like(coeffs)
 
@@ -250,18 +289,25 @@
     def _(b):
         at = rows_of(b)
         cols = base[at, :]
-        rest = x_all[at, :] - mm(cols, upper_ref[...])
+        rest = x_all[at, :] - mm_high(cols, upper_ref[...])
         x_all[at, :PANEL] = jnp.where(first, cols * norm, rest[:, :PANEL])
         x_all[at, PANEL:] = rest[:, PANEL:]
+
+    for k in range(1, n_row):
+        core_copy(k, 1 - core).wait_recv()
+
+    @pl.loop(0, n_row)
+    def _(b):
+        at = rows_of(b)
         live = mm_t(pts_all[b], pick_live)
         for k in range(panels):
             cut = slice(k * PANEL, (k + 1) * PANEL)
             upto = slice(0, (k + 1) * PANEL)
-            big_gram[cut, upto] += mm_t(v_all[at, cut] * live, v_all[at, upto])
+            big_gram[cut, upto] += mm_t_high(v_all[at, cut] * live, v_all[at, upto])
 
     def coefficients(b):
         at = rows_of(b)
-        coeffs[...] += mm_t(v_all[at, :], x_all[at, :])
+        coeffs[...] += mm_t_high(v_all[at, :], x_all[at, :])
 
     blocks_t = []
     inverses = []
@@ -297,7 +343,7 @@
             right = right - mm(big_gram[cut, :k * PANEL], coeffs[:k * PANEL, :])
         coeffs[cut, :] = mm(inverses[k], right)
     live = mm_t(pts_in[...], pick_live)
-    shift = mm(v_in[...], coeffs[...])
+    shift = mm_high(v_in[...], coeffs[...])
     at = rows_of(me)
     for q in range(width // PANEL):
         span = slice(q * PANEL, (q + 1) * PANEL)

time: 91 us -> 75.4 us (0.83)
  the two profiles are of different devices: /device:TPU:10 before, /device:TPU:0 now
where the time goes in v3:
time: 75.4 us; the launch traced here: 75.1 us
  Pallas kernels  68.9 us (91%)
  local copies, waits for them, and re-layouts  4.82 us (6%)
  between operations  1.39 us (2%)
    pallas_call x1, Pallas kernels, on_device(): pl.pallas_call(functools.partial(kernel, n_row, n_col), out_shape=(jax.Sh...  68.9 us
    unnamed x10, local copies, waits for them, and re-layouts  4.52 us

profile of v3, /device:TPU:0, one launch (start us, length us, event | category | flops | bytes accessed | tf_op | source)
XLA Modules:
  0.0 75.1 jit_solution(773225739192497948)
XLA Ops:
  1.3 0.0 copy-start.3
  1.3 0.7 copy-done.3
  2.0 0.0 copy-start.1
  2.0 0.7 copy-done.1
  2.7 0.0 copy-start.2
  2.7 0.7 copy-done.2
  3.4 0.1 broadcast_in_dim.3
  3.5 0.1 reshape.159
  3.7 0.0 copy-start
  3.7 1.0 %copy-done = f32[256,512]{1,0:T(8,128)S(1)} copy-done((f32[256,512]{1,0:T(8,128)S(1)}, f32[256,512]{1,0:T(8,128)}, u32[]{:S(2)}) %copy-start) | copy-done | bytes 524312
  4.8 68.9 %window.1 = (f32[256,512]{1,0:T(8,128)S(1)}, f32[128,512]{1,0:T(8,128)S(1)}) custom-call(f32[8,256]{1,0:T(8,128)S(1)} %stack.21.pts_in, f32[8,512]{1,0:T(8,128)S(1)} %stack.23.modes_ref, f32[256,512]{1,0:T(8,128)S(1)} %copy-done), custom_call_target="tpu_custom_call" | custom-call | tf_op jit(solution)/shard_map/window/pallas_call | solution.py:388
  73.6 0.8 %copy.10 = f32[256,512]{1,0:T(8,128)} copy(f32[256,512]{1,0:T(8,128)S(1)} %get-tuple-element.6) | data formatting | bytes 1048576
  74.4 0.7 copy.11
  (12 shorter events, 0.1 us)
Async XLA Ops:
  1.3 0.7 copy-start.3
  2.0 0.7 copy-start.1
  2.7 0.7 copy-start.2
  3.7 1.0 %copy-start = (f32[256,512]{1,0:T(8,128)S(1)}, f32[256,512]{1,0:T(8,128)}, u32[]{:S(2)}) copy-start(f32[256,512]{1,0:T(8,128)} %v_in.1) | copy-start | bytes 1572868
